TPU v7x, 32 devices: a whole 2x2x4 slice. The times are simulated.
32 devices in a mesh: cheb: 4 (over y, core), wear: 4 (over z), age: 2 (over x).
Axes of the slice: x: 2, y: 2, z: 4, core: 2. Of those that a mesh axis runs over, the one named last changes fastest.
Arguments:
- adjoint_value: float32 [256, 128, 1024], P('wear', 'age', 'cheb'), may hold values from -6 to 6
- load_diffusion: float32 [1024], replicated, may hold values from 0.2 to 1
- load_drift: float32 [1024], replicated, may hold values from -1 to 1
- wear_speed: float32 [1024], P('cheb'), may hold values from 0.05 to 0.3
- hazard: float32 [256, 128], P('wear', 'age'), may hold values from 0.05 to 0.5
Outputs:
- next_value: float32 [256, 128, 1024], P('wear', 'age', 'cheb')
All inputs are finite; a program needn't handle non-finite values.
Results may differ from a plain program's by a relative error of at most 0.0037.
Values may be sent and summed in bfloat16 or wider, within the bound.
No kernel may reach another device: no remote copies, remote signals or barrier semaphores. Data moves between devices by JAX's collectives and lax.ppermute only.
A program may use at most 128 MiB of HBM per device.

v0:
```python
import functools

import jax
import jax.numpy as jnp
import numpy as np
from jax import lax
from jax.experimental import pallas as pl
from jax.experimental.pallas import tpu as pltpu
from jax.sharding import PartitionSpec as P

SUBSTEPS = 4
HALO = SUBSTEPS

age_courant = 0.4
wear_spread = 0.1
coupling = 0.05
GAIN = 1.0 / coupling
START = coupling**SUBSTEPS

f32 = jnp.float32
bf16 = jnp.bfloat16
VMEM_LIMIT = 48 * 2**20


def operators(points):
    modes = np.arange(points)[:, None]
    nodes = np.arange(points)[None, :]
    angles = (modes * (2 * nodes + 1)) % (4 * points) * (np.pi / (2 * points))
    cosine, sine = np.cos(angles), np.sin(angles)
    analysis = np.where(modes == 0, 1.0, 2.0) / points * cosine
    wavenumber = modes / points
    return (-(wavenumber**2) * cosine).T @ analysis, (wavenumber * sine).T @ analysis


@functools.lru_cache(maxsize=None)
def factors(points, devices):
    second, first = operators(points)
    size = points // devices
    parts = [slice(b * size, (b + 1) * size) for b in range(devices)]
    slots, found = [], {}
    for shift in range(1, devices):
        groups = {}
        for c in range(devices):
            b = c ^ shift if devices & (devices - 1) == 0 else (c + shift) % devices
            joint = np.concatenate([second[parts[b], parts[c]], first[parts[b], parts[c]]])
            _, sizes, rows = np.linalg.svd(joint, full_matrices=False)
            rank = int((sizes > joint.shape[0] * np.finfo(np.float64).eps).sum())
            rank = -(-rank // 8) * 8
            basis = rows[:rank]
            found[c, b] = (basis, second[parts[b], parts[c]] @ basis.T, first[parts[b], parts[c]] @ basis.T)
            groups.setdefault(rank, []).append((c, b))
        slots += [(tuple(pairs), rank) for rank, pairs in sorted(groups.items())]
    total = sum(rank for _, rank in slots)
    send = np.zeros((devices, total, size))
    take_second = np.zeros((devices, total, size))
    take_first = np.zeros((devices, total, size))
    at = 0
    for pairs, rank in slots:
        for c, b in pairs:
            basis, left_second, left_first = found[c, b]
            send[c, at : at + rank] = basis
            take_second[b, at : at + rank] = left_second.T
            take_first[b, at : at + rank] = left_first.T
        at += rank
    own_second = np.stack([second[p, p].T for p in parts])
    own_first = np.stack([first[p, p].T for p in parts])
    return slots, send, take_second, take_first, own_second, own_first


def pack_kernel(ranks, at_ref, u_ref, send_ref, *out_refs):
    halves = []
    for half in range(2):
        cells = u_ref[half].reshape(-1, u_ref.shape[-1]).astype(bf16)
        halves.append(
            lax.dot_general(send_ref[0], cells, (((1,), (1,)), ((), ())), preferred_element_type=f32)
        )
    row = 0
    for rank, out_ref in zip(ranks, out_refs):
        both = jnp.concatenate([h[row : row + rank] for h in halves], axis=0)
        out_ref[...] = both.astype(bf16)
        row += rank


def pack(at, u4, send, ranks, chunk):
    _, wears, ages, size = u4.shape
    cells = wears * ages
    return pl.pallas_call(
        functools.partial(pack_kernel, ranks),
        grid_spec=pltpu.PrefetchScalarGridSpec(
            num_scalar_prefetch=1,
            grid=(wears // chunk,),
            in_specs=[
                pl.BlockSpec((2, chunk, ages, size), lambda g, at: (0, g, 0, 0)),
                pl.BlockSpec((1, sum(ranks), size), lambda g, at: (at[0], 0, 0)),
            ],
            out_specs=[pl.BlockSpec((2 * r, chunk * ages), lambda g, at: (0, g)) for r in ranks],
        ),
        out_shape=[jax.ShapeDtypeStruct((2 * r, cells), bf16) for r in ranks],
        compiler_params=pltpu.CompilerParams(vmem_limit_bytes=VMEM_LIMIT),
        cost_estimate=pl.CostEstimate(
            flops=4 * cells * sum(ranks) * size, bytes_accessed=8 * cells * size, transcendentals=0
        ),
        name="pack_coefficients",
    )(at, u4, send)


def section_kernel(ranks, sides, at_ref, side_ref, u_ref, keep_ref, second_ref, first_ref, take_second_ref,
                   take_first_ref, diffusion_ref, drift_ref, *refs):
    q_refs, refs = refs[: len(ranks)], refs[len(ranks) :]
    s_ref, top_ref, bottom_ref = refs[:3]
    edge_refs = refs[3 : 3 + sides]
    own, take = refs[3 + sides :]
    g = pl.program_id(0)
    chunk, ages, size = u_ref.shape[1:]

    @pl.when(g == 0)
    def _():
        diffusion, drift = diffusion_ref[0] * START, drift_ref[0] * START
        own[...] = (second_ref[0] * diffusion + first_ref[0] * drift).astype(bf16)
        take[...] = (take_second_ref[0] * diffusion + take_first_ref[0] * drift).astype(bf16)

    for half in range(2):
        u = u_ref[half].reshape(chunk * ages, size)
        rate = jnp.dot(u.astype(bf16), own[...], preferred_element_type=f32)
        q = jnp.concatenate([r[...].astype(f32)[half * n : half * n + n] for r, n in zip(q_refs, ranks)], axis=0)
        rate += lax.dot_general(
            q.astype(bf16), take[...], (((0,), (0,)), ((), ())), preferred_element_type=f32
        )
        keep = keep_ref[half].reshape(chunk * ages, 128)
        sectioned = rate + jnp.concatenate(
            [keep * u[:, i : i + 128] for i in range(0, size, 128)], axis=1
        )
        sectioned = sectioned.reshape(chunk, ages, size)
        s_ref[half] = sectioned
        last = [sectioned[w, ages - HALO :] for w in range(chunk)]
        first = [sectioned[w, :HALO] for w in range(chunk)]
        last, first = jnp.concatenate(last, axis=0), jnp.concatenate(first, axis=0)
        if sides == 1:
            edge_refs[0][half] = jnp.where(side_ref[0] == 0, last, first).astype(bf16)
        else:
            edge_refs[0][half] = last.astype(bf16)
            edge_refs[1][half] = first.astype(bf16)
        if half == 0:
            @pl.when(g == 0)
            def _():
                top_ref[...] = sectioned[:HALO].reshape(HALO * ages, size).astype(bf16)
        else:
            @pl.when(g == pl.num_programs(0) - 1)
            def _():
                bottom_ref[...] = sectioned[chunk - HALO :].reshape(HALO * ages, size).astype(bf16)


def section(at, side, u4, keep, tables, diffusion, drift, q, ranks, sides, chunk):
    _, wears, ages, size = u4.shape
    cells = wears * ages
    own_second, own_first, take_second, take_first = tables
    total = sum(ranks)
    mine = lambda g, at, side: (at[0], 0, 0)
    whole = lambda g, at, side: (0, 0)
    return pl.pallas_call(
        functools.partial(section_kernel, ranks, sides),
        grid_spec=pltpu.PrefetchScalarGridSpec(
            num_scalar_prefetch=2,
            grid=(wears // chunk,),
            in_specs=[
                pl.BlockSpec((2, chunk, ages, size), lambda g, at, side: (0, g, 0, 0)),
                pl.BlockSpec((2, chunk, ages, 128), lambda g, at, side: (0, g, 0, 0)),
                pl.BlockSpec((1, size, size), mine),
                pl.BlockSpec((1, size, size), mine),
                pl.BlockSpec((1, total, size), mine),
                pl.BlockSpec((1, total, size), mine),
                pl.BlockSpec((1, 1, size), mine),
                pl.BlockSpec((1, 1, size), mine),
            ]
            + [pl.BlockSpec((2 * r, chunk * ages), lambda g, at, side: (0, g)) for r in ranks],
            out_specs=[
                pl.BlockSpec((2, chunk, ages, size), lambda g, at, side: (0, g, 0, 0)),
                pl.BlockSpec((HALO * ages, size), whole),
                pl.BlockSpec((HALO * ages, size), whole),
            ]
            + [pl.BlockSpec((2, chunk * HALO, size), lambda g, at, side: (0, g, 0))] * sides,
            scratch_shapes=[pltpu.VMEM((size, size), bf16), pltpu.VMEM((total, size), bf16)],
        ),
        out_shape=[
            jax.ShapeDtypeStruct((2, wears, ages, size), f32),
            jax.ShapeDtypeStruct((HALO * ages, size), bf16),
            jax.ShapeDtypeStruct((HALO * ages, size), bf16),
        ]
        + [jax.ShapeDtypeStruct((2, wears * HALO, size), bf16)] * sides,
        compiler_params=pltpu.CompilerParams(vmem_limit_bytes=VMEM_LIMIT),
        cost_estimate=pl.CostEstimate(
            flops=4 * cells * (total + size) * size, bytes_accessed=24 * cells * size, transcendentals=0
        ),
        name="section",
    )(at, side, u4, keep, own_second, own_first, take_second, take_first, diffusion, drift, *q)


ROW0 = 16


def substeps_kernel(flag_ref, s_ref, speed_ref, up_ref, down_ref, left_ref, right_ref, ul_ref, ur_ref, dl_ref,
                    dr_ref, o_ref, za, zb, stage, in_sem, out_sem):
    halves, rows, _, _ = za.shape
    wears, ages = rows - 2 * HALO, stage.shape[1]
    first_w, last_w, first_a, last_a = (flag_ref[i] == 1 for i in range(4))
    low, high = ROW0 - 8, ROW0 + ages + 8
    loads = []
    for l in range(halves):
        copy = pltpu.make_async_copy(
            s_ref.at[:, :, pl.ds(l * 128, 128)],
            za.at[l, pl.ds(HALO, wears), pl.ds(ROW0, ages), :],
            in_sem.at[l],
        )
        copy.start()
        loads.append(copy)
    has_left = jnp.where(first_a, 0.0, 1.0).astype(f32)
    has_right = jnp.where(last_a, 0.0, 1.0).astype(f32)
    for l in range(halves):
        lanes = pl.ds(l * 128, 128)
        zero = jnp.zeros((rows, 8, 128), f32)
        za[l, :, low:ROW0, :] = zero
        za[l, :, ROW0 + ages : high, :] = zero
        for z in (za, zb):
            z[l, :, low - 8 : low, :] = zero
            z[l, :, high : high + 8, :] = zero
        for ref, at, wide in ((up_ref, 0, None), (down_ref, HALO + wears, None)):
            za[l, at : at + HALO, ROW0 : ROW0 + ages, :] = ref[:, lanes].astype(f32).reshape(HALO, ages, 128)
        for ref, at, count, col, has in (
            (left_ref, HALO, wears, ROW0 - HALO, has_left),
            (right_ref, HALO, wears, ROW0 + ages, has_right),
            (ul_ref, 0, HALO, ROW0 - HALO, has_left),
            (ur_ref, 0, HALO, ROW0 + ages, has_right),
            (dl_ref, HALO + wears, HALO, ROW0 - HALO, has_left),
            (dr_ref, HALO + wears, HALO, ROW0 + ages, has_right),
        ):
            strip = ref[:, lanes].astype(f32) * has
            za[l, at : at + count, col : col + HALO, :] = strip.reshape(count, HALO, 128)
    sublane = lax.broadcasted_iota(jnp.int32, (8, 128), 0)
    for copy in loads:
        copy.wait()

    keep_low = jnp.zeros((8, 128), f32) + has_left
    keep_high = jnp.zeros((8, 128), f32) + has_right
    stores = []
    for k in range(1, SUBSTEPS + 1):
        src, dst = (za, zb) if k % 2 == 1 else (zb, za)
        final = k == SUBSTEPS
        lo, hi = (ROW0, ROW0 + ages) if final else (low, high)
        pieces = 4 if final else 1
        bounds = [k + (rows - 2 * k) * p // pieces for p in range(pieces + 1)]
        for p in range(pieces):
            for l in range(halves):
                speed = speed_ref[0:1, l * 128 : (l + 1) * 128]
                stay = GAIN * (1.0 - age_courant - 2.0 * wear_spread - speed)
                worn = GAIN * (speed + wear_spread)

                def terms(w, src=src, l=l, lo=lo, hi=hi, stay=stay, worn=worn):
                    t = src[l, w, lo:hi, :]
                    older = src[l, w, lo + 1 : hi + 1, :]
                    slope = older - src[l, w, lo - 1 : hi - 1, :]
                    centre = stay * t + (GAIN * age_courant) * older
                    less = (t - slope) + t
                    return centre, worn * t + slope, less

                def body(w, carry, dst=dst, l=l, lo=lo, hi=hi, final=final, terms=terms):
                    partial, less = carry
                    centre, more, new_less = terms(w + 1)
                    out = partial + more
                    if final:
                        stage[w - HALO, :, l * 128 : (l + 1) * 128] = out
                    else:
                        dst[l, w, lo : lo + 8, :] = out[:8] * keep_low
                        dst[l, w, lo + 8 : hi - 8, :] = out[8:-8]
                        dst[l, w, hi - 8 : hi, :] = out[-8:] * keep_high
                    return centre + less, new_less

                start, stop = bounds[p], bounds[p + 1]
                _, _, less0 = terms(start - 1)
                centre1, _, less1 = terms(start)
                count = stop - start
                lax.fori_loop(start, stop, body, (centre1 + less0, less1), unroll=4 if count % 4 == 0 else 2)
            if final:
                a, b = bounds[p] - HALO, bounds[p + 1] - HALO
                copy = pltpu.make_async_copy(
                    stage.at[pl.ds(a, b - a)], o_ref.at[pl.ds(a, b - a)], out_sem.at[p]
                )
                copy.start()
                stores.append(copy)
        if not final:
            for at, flag in ((HALO - 1, first_w), (HALO + wears, last_w)):
                @pl.when(flag)
                def _(dst=dst, at=at):
                    for l in range(halves):
                        dst[l, at, low:high, :] = jnp.zeros((high - low, 128), f32)
    for copy in stores:
        copy.wait()


def run_substeps(flags, s, speed, halos):
    wears, ages, size = s.shape
    halves = size // 128
    rows = wears + 2 * HALO
    vmem = pl.BlockSpec(memory_space=pltpu.VMEM)
    buffer = pltpu.VMEM((halves, rows, ages + 32, 128), f32)
    return pl.pallas_call(
        substeps_kernel,
        out_shape=jax.ShapeDtypeStruct(s.shape, f32),
        in_specs=[pl.BlockSpec(memory_space=pltpu.SMEM), pl.BlockSpec(memory_space=pl.ANY)] + [vmem] * 9,
        out_specs=pl.BlockSpec(memory_space=pl.ANY),
        scratch_shapes=[
            buffer,
            buffer,
            pltpu.VMEM(s.shape, f32),
            pltpu.SemaphoreType.DMA((halves,)),
            pltpu.SemaphoreType.DMA((4,)),
        ],
        compiler_params=pltpu.CompilerParams(vmem_limit_bytes=VMEM_LIMIT),
        cost_estimate=pl.CostEstimate(
            flops=10 * SUBSTEPS * wears * ages * size, bytes_accessed=8 * wears * ages * size, transcendentals=0
        ),
        name="substeps",
    )(flags, s, speed, *halos)


def body(adjoint_value, load_diffusion, load_drift, wear_speed, hazard):
    wears, ages, size = adjoint_value.shape
    points = load_diffusion.shape[0]
    devices = points // size
    slots, send, take_second, take_first, own_second, own_first = factors(points, devices)
    ranks = tuple(rank for _, rank in slots)
    cheb = lax.axis_index("cheb")
    wear, age = lax.axis_index("wear"), lax.axis_index("age")
    n_wear, n_age = lax.axis_size("wear"), lax.axis_size("age")
    at = cheb.astype(jnp.int32).reshape(1)
    side = age.astype(jnp.int32).reshape(1)
    u4 = adjoint_value.reshape(2, wears // 2, ages, size)
    chunk = 4

    q = pack(at, u4, jnp.asarray(send, bf16), ranks, chunk)
    arrived = [lax.ppermute(x, "cheb", list(pairs)) for x, (pairs, _) in zip(q, slots)]

    keep = jnp.broadcast_to((START * (1.0 - hazard))[:, :, None], (wears, ages, 128))
    keep = keep.reshape(2, wears // 2, ages, 128)
    tables = [jnp.asarray(t, f32) for t in (own_second, own_first, take_second, take_first)]
    sides = 1 if n_age == 2 else 2
    out = section(
        at, side, u4, keep, tables, load_diffusion.reshape(devices, 1, size), load_drift.reshape(devices, 1, size),
        arrived, ranks, sides, chunk,
    )
    s, top, bottom = out[:3]
    edges = out[3:]
    s = s.reshape(wears, ages, size)
    corner = HALO * HALO

    def shift(x, dw, da):
        pairs = []
        for w in range(n_wear):
            for a in range(n_age):
                to_w, to_a = w + dw, (1 - a if da is None else a + da)
                if 0 <= to_w < n_wear and 0 <= to_a < n_age:
                    pairs.append((w * n_age + a, to_w * n_age + to_a))
        return lax.ppermute(x, ("wear", "age"), pairs)

    up, down = shift(bottom, 1, 0), shift(top, -1, 0)
    if sides == 1:
        x = edges[0]
        left = right = shift(x, 0, None).reshape(-1, size)
        ul = ur = shift(x[1, -corner:], 1, None)
        dl = dr = shift(x[0, :corner], -1, None)
    else:
        last, first = edges
        left, right = shift(last, 0, 1).reshape(-1, size), shift(first, 0, -1).reshape(-1, size)
        ul, ur = shift(last[1, -corner:], 1, 1), shift(first[1, -corner:], 1, -1)
        dl, dr = shift(last[0, :corner], -1, 1), shift(first[0, :corner], -1, -1)
    flags = jnp.stack([wear == 0, wear == n_wear - 1, age == 0, age == n_age - 1]).astype(jnp.int32)
    halos = [up, down, left, right, ul, ur, dl, dr]
    return run_substeps(flags, s, wear_speed.reshape(1, size), halos)


def solution(mesh):
    placed = (P("wear", "age", "cheb"), P(), P(), P("cheb"), P("wear", "age"))
    return jax.shard_map(
        body, mesh=mesh, in_specs=placed, out_specs=P("wear", "age", "cheb"), check_vma=False
    )
```

profile of v0, /device:TPU:22, one launch (start us, length us, event | category | flops | bytes accessed | tf_op | source)
XLA Modules:
  0.0 57.5 jit_solution(2070464008804963250)
XLA Ops:
  0.0 0.0 copy-start.8
  0.0 0.0 copy-start.7
  0.0 0.0 copy-start
  0.0 2.2 %copy-done = f32[64,64,256]{2,1,0:T(8,128)S(1)} copy-done((f32[64,64,256]{2,1,0:T(8,128)S(1)}, f32[64,64,256]{2,1,0:T(8,128)}, u32[]{:S(2)}) %copy-start) | copy-done | bytes 4194328
  2.2 0.0 copy-start.6
  2.2 0.9 %copy-done.6 = bf16[4,64,256]{2,1,0:T(8,128)(2,1)S(1)} copy-done((bf16[4,64,256]{2,1,0:T(8,128)(2,1)S(1)}, bf16[4,64,256]{2,1,0:T(8,128)(2,1)}, u32[]{:S(2)}) %copy-start.6) | copy-done | bytes 131096
  3.1 0.0 copy-start.10
  3.1 0.0 copy-start.2
  3.1 0.0 copy-start.3
  3.1 0.0 copy-start.4
  3.1 0.0 copy-start.5
  3.1 3.7 %pack_coefficients.1 = (bf16[48,2048]{1,0:T(8,128)(2,1)S(1)}, bf16[16,2048]{1,0:T(8,128)(2,1)}, bf16[16,2048]{1,0:T(8,128)(2,1)}, bf16[48,2048]{1,0:T(8,128)(2,1)S(1)}) custom-call(s32[1]{0:T(128)} %bitcast.4.at_ref, f32[2,32,64,256]{3,2,1,0:T(8,128)S(1)} %bitcast.18, bf16[4,64,256]{2,1,0:T(8,128)(2,1)S(1)} %copy-done.6), custom_call_target="tpu_custom_call" | custom-call | flops 134217728 | bytes 4194304 | tf_op jit(solution)/shard_map/pack_coefficients/pallas_call | solution.py:87
  6.8 0.5 collective-permute-start.1
  7.3 0.7 %collective-permute-start.2 = (bf16[16,2048]{1,0:T(8,128)(2,1)}, bf16[16,2048]{1,0:T(8,128)(2,1)S(1)}, u32[]{:S(2)}, u32[]{:S(2)}) collective-permute-start(bf16[16,2048]{1,0:T(8,128)(2,1)} %get-tuple-element.15), channel_id=1, source_target_pairs={{0,24},{24,0},{1,25},{25,1},{2,26},{26,2},{3,27},{27,3},{4,28},{28... | collective-permute-start | bytes 196616 | tf_op jit(solution)/shard_map/ppermute | solution.py:340
  8.0 2.9 %collective-permute-start = (bf16[48,2048]{1,0:T(8,128)(2,1)S(1)}, bf16[48,2048]{1,0:T(8,128)(2,1)S(1)}, u32[]{:S(2)}, u32[]{:S(2)}) collective-permute-start(bf16[48,2048]{1,0:T(8,128)(2,1)S(1)} %get-tuple-element.13), channel_id=1, source_target_pairs={{0,8},{8,0},{16,24},{24,16},{1,9},{9,1},{17,25},{25,17},{2,10},{10... | collective-permute-start | bytes 589832 | tf_op jit(solution)/shard_map/ppermute | solution.py:340
  11.0 1.9 %collective-permute-start.3 = (bf16[48,2048]{1,0:T(8,128)(2,1)S(1)}, bf16[48,2048]{1,0:T(8,128)(2,1)S(1)}, u32[]{:S(2)}, u32[]{:S(2)}) collective-permute-start(bf16[48,2048]{1,0:T(8,128)(2,1)S(1)} %get-tuple-element.16), channel_id=1, source_target_pairs={{8,16},{16,8},{9,17},{17,9},{10,18},{18,10},{11,19},{19,11},{12,20... | collective-permute-start | bytes 589832 | tf_op jit(solution)/shard_map/ppermute | solution.py:340
  12.9 0.0 copy-done.10
  12.9 0.6 %subtract_multiply_fusion = f32[64,64]{1,0:T(8,128)} fusion(f32[64,64]{1,0:T(8,128)S(1)} %copy-done.10), kind=kLoop, calls=%fused_computation | loop fusion | flops 8192 | bytes 32768 | tf_op jit(solution)/shard_map/mul | solution.py:342
  13.5 0.0 collective-permute-done.1.refs_1_
  13.5 0.0 collective-permute-done.2.refs_2_
  13.5 0.0 collective-permute-done.refs_0_
  13.5 4.4 %collective-permute-done.3.refs_3_ = bf16[48,2048]{1,0:T(8,128)(2,1)S(1)} collective-permute-done((bf16[48,2048]{1,0:T(8,128)(2,1)S(1)}, bf16[48,2048]{1,0:T(8,128)(2,1)S(1)}, u32[]{:S(2)}, u32[]{:S(2)}) %collective-permute-start.3) | collective-permute-done | bytes 196640 | tf_op jit(solution)/shard_map/ppermute | solution.py:340
  17.9 1.4 %broadcast_in_dim.9.keep_ref = f32[2,32,64,128]{3,2,1,0:T(8,128)S(1)} broadcast(f32[2,32,64]{2,1,0:T(8,128)} %bitcast.25), dimensions={0,1,2} | broadcast | bytes 2113536 | tf_op jit(solution)/shard_map/broadcast_in_dim | solution.py:342
  19.3 0.0 copy-done.8
  19.3 0.0 copy-done.7
  19.3 0.0 copy-done.2
  19.3 0.0 copy-done.3
  19.3 0.0 copy-done.4
  19.3 0.0 copy-done.5
  19.4 0.0 copy-start.9
  19.4 9.0 %section.1 = (f32[2,32,64,256]{3,2,1,0:T(8,128)}, bf16[256,256]{1,0:T(8,128)(2,1)S(1)}, bf16[256,256]{1,0:T(8,128)(2,1)S(1)}, bf16[2,128,256]{2,1,0:T(8,128)(2,1)S(1)}) custom-call(s32[1]{0:T(128)} %bitcast.4.at_ref, s32[1]{0:T(128)} %bitcast.5.side_ref, f32[2,32,64,256]{3,2,1,0:T(8,128)} %bitcast.17, f32[2,32,64,128]{3,2,1,0:T(8,128)S(1)} %broadcast_in_dim.9.keep_ref, ...), custom_call_target="tpu_custom_call" | custom-call | flops 671088640 | bytes 12582912 | tf_op jit(solution)/shard_map/section/pallas_call | solution.py:160
  28.3 3.5 %collective-permute-start.4 = (bf16[256,256]{1,0:T(8,128)(2,1)S(1)}, bf16[256,256]{1,0:T(8,128)(2,1)S(1)}, u32[]{:S(2)}, u32[]{:S(2)}) collective-permute-start(bf16[256,256]{1,0:T(8,128)(2,1)S(1)} %get-tuple-element.18), channel_id=1, source_target_pairs={{0,2},{1,3},{2,4},{3,5},{4,6},{5,7},{8,10},{9,11},{10,12},{11,13},... | collective-permute-start | bytes 393224 | tf_op jit(solution)/shard_map/ppermute | solution.py:362
  31.8 2.4 %collective-permute-start.5 = (bf16[256,256]{1,0:T(8,128)(2,1)S(1)}, bf16[256,256]{1,0:T(8,128)(2,1)S(1)}, u32[]{:S(2)}, u32[]{:S(2)}) collective-permute-start(bf16[256,256]{1,0:T(8,128)(2,1)S(1)} %get-tuple-element.19), channel_id=1, source_target_pairs={{2,0},{3,1},{4,2},{5,3},{6,4},{7,5},{10,8},{11,9},{12,10},{13,11},... | collective-permute-start | bytes 393224 | tf_op jit(solution)/shard_map/ppermute | solution.py:362
  34.2 0.6 %collective-permute-start.6 = (bf16[2,128,256]{2,1,0:T(8,128)(2,1)S(1)}, bf16[2,128,256]{2,1,0:T(8,128)(2,1)S(1)}, u32[]{:S(2)}, u32[]{:S(2)}) collective-permute-start(bf16[2,128,256]{2,1,0:T(8,128)(2,1)S(1)} %get-tuple-element.20), channel_id=1, source_target_pairs={{0,1},{1,0},{2,3},{3,2},{4,5},{5,4},{6,7},{7,6},{8,9},{9,8},{10,11... | collective-permute-start | bytes 393224 | tf_op jit(solution)/shard_map/ppermute | solution.py:362
  34.8 3.3 %collective-permute-start.8 = (bf16[16,256]{1,0:T(8,128)(2,1)S(1)}, bf16[16,256]{1,0:T(8,128)(2,1)S(1)}, u32[]{:S(2)}, u32[]{:S(2)}) collective-permute-start(bf16[16,256]{1,0:T(8,128)(2,1)S(1)} %get-tuple-element.21), channel_id=1, source_target_pairs={{2,1},{3,0},{4,3},{5,2},{6,5},{7,4},{10,9},{11,8},{12,11},{13,10},... | collective-permute-start | bytes 24584 | tf_op jit(solution)/shard_map/ppermute | solution.py:362
  38.1 3.4 %collective-permute-start.7 = (bf16[16,256]{1,0:T(8,128)(2,1)S(1)}, bf16[16,256]{1,0:T(8,128)(2,1)S(1)}, u32[]{:S(2)}, u32[]{:S(2)}) collective-permute-start(bf16[16,256]{1,0:T(8,128)(2,1)S(1)} %get-tuple-element.22), channel_id=1, source_target_pairs={{0,3},{1,2},{2,5},{3,4},{4,7},{5,6},{8,11},{9,10},{10,13},{11,12},... | collective-permute-start | bytes 24584 | tf_op jit(solution)/shard_map/ppermute | solution.py:362
  41.5 0.1 add_convert_fusion.flag_ref
  41.6 0.0 collective-permute-done.8.dl_ref.dr_ref
  41.6 2.9 %collective-permute-done.7.ul_ref.ur_ref = bf16[16,256]{1,0:T(8,128)(2,1)S(1)} collective-permute-done((bf16[16,256]{1,0:T(8,128)(2,1)S(1)}, bf16[16,256]{1,0:T(8,128)(2,1)S(1)}, u32[]{:S(2)}, u32[]{:S(2)}) %collective-permute-start.7) | collective-permute-done | bytes 8224 | tf_op jit(solution)/shard_map/ppermute | solution.py:362
  44.5 0.0 collective-permute-done.4.up_ref
  44.5 0.0 collective-permute-done.5.down_ref
  44.5 0.0 collective-permute-done.6
  44.5 0.0 copy-done.9
  44.5 0.0 copy-start.1
  44.5 2.2 %copy-done.1 = f32[2,32,64,256]{3,2,1,0:T(8,128)S(1)} copy-done((f32[2,32,64,256]{3,2,1,0:T(8,128)S(1)}, f32[2,32,64,256]{3,2,1,0:T(8,128)}, u32[]{:S(2)}) %copy-start.1) | copy-done | bytes 4194328
  46.7 10.8 %substeps.1 = f32[64,64,256]{2,1,0:T(8,128)} custom-call(s32[4]{0:T(128)S(1)} %add_convert_fusion.flag_ref, f32[64,64,256]{2,1,0:T(8,128)S(1)} %bitcast.19, f32[1,256]{1,0:T(1,128)S(1)} %bitcast.24, bf16[256,256]{1,0:T(8,128)(2,1)S(1)} %collective-permute-done.4.up_ref, bf16[256,256]{1,0:T(8,128)(2,1)S(1)} %collective-permute-done.5.down_ref, ...), custom_call_target="tpu_custom_call" | custom-call | flops 41943040 | bytes 8388608 | tf_op jit(solution)/shard_map/substeps/pallas_call | solution.py:305
  (1 shorter events, 0.0 us)
Async XLA Ops:
  0.0 19.3 %copy-start.8 = (f32[1024]{0:T(1024)S(1)}, f32[1024]{0:T(1024)}, u32[]{:S(2)}) copy-start(f32[1024]{0:T(1024)} %param.12) | copy-start | bytes 12292
  0.0 19.3 %copy-start.7 = (f32[1024]{0:T(1024)S(1)}, f32[1024]{0:T(1024)}, u32[]{:S(2)}) copy-start(f32[1024]{0:T(1024)} %param.11) | copy-start | bytes 12292
  0.0 2.2 %copy-start = (f32[64,64,256]{2,1,0:T(8,128)S(1)}, f32[64,64,256]{2,1,0:T(8,128)}, u32[]{:S(2)}) copy-start(f32[64,64,256]{2,1,0:T(8,128)} %param.10) | copy-start | bytes 12582916
  2.2 0.9 %copy-start.6 = (bf16[4,64,256]{2,1,0:T(8,128)(2,1)S(1)}, bf16[4,64,256]{2,1,0:T(8,128)(2,1)}, u32[]{:S(2)}) copy-start(bf16[4,64,256]{2,1,0:T(8,128)(2,1)} %constant.31.clone.send_ref) | copy-start | bytes 393220
  3.1 9.7 %copy-start.10 = (f32[64,64]{1,0:T(8,128)S(1)}, f32[64,64]{1,0:T(8,128)}, u32[]{:S(2)}) copy-start(f32[64,64]{1,0:T(8,128)} %param.14) | copy-start | bytes 49156
  3.1 16.2 %copy-start.2 = (f32[4,256,256]{2,1,0:T(8,128)S(1)}, f32[4,256,256]{2,1,0:T(8,128)}, u32[]{:S(2)}) copy-start(f32[4,256,256]{2,1,0:T(8,128)} %constant.33.clone.first_ref) | copy-start | bytes 3145732
  3.1 16.2 %copy-start.3 = (f32[4,256,256]{2,1,0:T(8,128)S(1)}, f32[4,256,256]{2,1,0:T(8,128)}, u32[]{:S(2)}) copy-start(f32[4,256,256]{2,1,0:T(8,128)} %constant.32.clone.second_ref) | copy-start | bytes 3145732
  3.1 16.2 %copy-start.4 = (f32[4,64,256]{2,1,0:T(8,128)S(1)}, f32[4,64,256]{2,1,0:T(8,128)}, u32[]{:S(2)}) copy-start(f32[4,64,256]{2,1,0:T(8,128)} %constant.35.clone.take_first_ref) | copy-start | bytes 786436
  3.1 16.2 %copy-start.5 = (f32[4,64,256]{2,1,0:T(8,128)S(1)}, f32[4,64,256]{2,1,0:T(8,128)}, u32[]{:S(2)}) copy-start(f32[4,64,256]{2,1,0:T(8,128)} %constant.34.clone.take_second_ref) | copy-start | bytes 786436
  6.8 6.7 %collective-permute-start.1 = (bf16[16,2048]{1,0:T(8,128)(2,1)}, bf16[16,2048]{1,0:T(8,128)(2,1)S(1)}, u32[]{:S(2)}, u32[]{:S(2)}) collective-permute-start(bf16[16,2048]{1,0:T(8,128)(2,1)} %get-tuple-element.14), channel_id=1, source_target_pairs={{0,16},{8,24},{16,0},{24,8},{1,17},{9,25},{17,1},{25,9},{2,18},{10... | collective-permute-start | bytes 196616 | tf_op jit(solution)/shard_map/ppermute | solution.py:340
  7.3 6.2 %collective-permute-start.2 = (bf16[16,2048]{1,0:T(8,128)(2,1)}, bf16[16,2048]{1,0:T(8,128)(2,1)S(1)}, u32[]{:S(2)}, u32[]{:S(2)}) collective-permute-start(bf16[16,2048]{1,0:T(8,128)(2,1)} %get-tuple-element.15), channel_id=1, source_target_pairs={{0,24},{24,0},{1,25},{25,1},{2,26},{26,2},{3,27},{27,3},{4,28},{28... | collective-permute-start | bytes 196616 | tf_op jit(solution)/shard_map/ppermute | solution.py:340
  8.0 5.5 %collective-permute-start = (bf16[48,2048]{1,0:T(8,128)(2,1)S(1)}, bf16[48,2048]{1,0:T(8,128)(2,1)S(1)}, u32[]{:S(2)}, u32[]{:S(2)}) collective-permute-start(bf16[48,2048]{1,0:T(8,128)(2,1)S(1)} %get-tuple-element.13), channel_id=1, source_target_pairs={{0,8},{8,0},{16,24},{24,16},{1,9},{9,1},{17,25},{25,17},{2,10},{10... | collective-permute-start | bytes 589832 | tf_op jit(solution)/shard_map/ppermute | solution.py:340
  11.0 7.0 %collective-permute-start.3 = (bf16[48,2048]{1,0:T(8,128)(2,1)S(1)}, bf16[48,2048]{1,0:T(8,128)(2,1)S(1)}, u32[]{:S(2)}, u32[]{:S(2)}) collective-permute-start(bf16[48,2048]{1,0:T(8,128)(2,1)S(1)} %get-tuple-element.16), channel_id=1, source_target_pairs={{8,16},{16,8},{9,17},{17,9},{10,18},{18,10},{11,19},{19,11},{12,20... | collective-permute-start | bytes 589832 | tf_op jit(solution)/shard_map/ppermute | solution.py:340
  19.4 25.2 %copy-start.9 = (f32[256]{0:T(256)S(1)}, f32[256]{0:T(256)}, u32[]{:S(2)}) copy-start(f32[256]{0:T(256)} %param.13) | copy-start | bytes 3076
  28.3 16.2 %collective-permute-start.4 = (bf16[256,256]{1,0:T(8,128)(2,1)S(1)}, bf16[256,256]{1,0:T(8,128)(2,1)S(1)}, u32[]{:S(2)}, u32[]{:S(2)}) collective-permute-start(bf16[256,256]{1,0:T(8,128)(2,1)S(1)} %get-tuple-element.18), channel_id=1, source_target_pairs={{0,2},{1,3},{2,4},{3,5},{4,6},{5,7},{8,10},{9,11},{10,12},{11,13},... | collective-permute-start | bytes 393224 | tf_op jit(solution)/shard_map/ppermute | solution.py:362
  31.8 12.7 %collective-permute-start.5 = (bf16[256,256]{1,0:T(8,128)(2,1)S(1)}, bf16[256,256]{1,0:T(8,128)(2,1)S(1)}, u32[]{:S(2)}, u32[]{:S(2)}) collective-permute-start(bf16[256,256]{1,0:T(8,128)(2,1)S(1)} %get-tuple-element.19), channel_id=1, source_target_pairs={{2,0},{3,1},{4,2},{5,3},{6,4},{7,5},{10,8},{11,9},{12,10},{13,11},... | collective-permute-start | bytes 393224 | tf_op jit(solution)/shard_map/ppermute | solution.py:362
  34.2 10.3 %collective-permute-start.6 = (bf16[2,128,256]{2,1,0:T(8,128)(2,1)S(1)}, bf16[2,128,256]{2,1,0:T(8,128)(2,1)S(1)}, u32[]{:S(2)}, u32[]{:S(2)}) collective-permute-start(bf16[2,128,256]{2,1,0:T(8,128)(2,1)S(1)} %get-tuple-element.20), channel_id=1, source_target_pairs={{0,1},{1,0},{2,3},{3,2},{4,5},{5,4},{6,7},{7,6},{8,9},{9,8},{10,11... | collective-permute-start | bytes 393224 | tf_op jit(solution)/shard_map/ppermute | solution.py:362
  34.8 6.8 %collective-permute-start.8 = (bf16[16,256]{1,0:T(8,128)(2,1)S(1)}, bf16[16,256]{1,0:T(8,128)(2,1)S(1)}, u32[]{:S(2)}, u32[]{:S(2)}) collective-permute-start(bf16[16,256]{1,0:T(8,128)(2,1)S(1)} %get-tuple-element.21), channel_id=1, source_target_pairs={{2,1},{3,0},{4,3},{5,2},{6,5},{7,4},{10,9},{11,8},{12,11},{13,10},... | collective-permute-start | bytes 24584 | tf_op jit(solution)/shard_map/ppermute | solution.py:362
  38.1 6.4 %collective-permute-start.7 = (bf16[16,256]{1,0:T(8,128)(2,1)S(1)}, bf16[16,256]{1,0:T(8,128)(2,1)S(1)}, u32[]{:S(2)}, u32[]{:S(2)}) collective-permute-start(bf16[16,256]{1,0:T(8,128)(2,1)S(1)} %get-tuple-element.22), channel_id=1, source_target_pairs={{0,3},{1,2},{2,5},{3,4},{4,7},{5,6},{8,11},{9,10},{10,13},{11,12},... | collective-permute-start | bytes 24584 | tf_op jit(solution)/shard_map/ppermute | solution.py:362
  44.5 2.2 %copy-start.1 = (f32[2,32,64,256]{3,2,1,0:T(8,128)S(1)}, f32[2,32,64,256]{3,2,1,0:T(8,128)}, u32[]{:S(2)}) copy-start(f32[2,32,64,256]{3,2,1,0:T(8,128)} %get-tuple-element.17) | copy-start | bytes 12582916
where the time goes:
time: 58.1 us; the launch traced here: 57.5 us
  Pallas kernels  23.5 us (40%)
  starting transfers between devices  19.2 us (33%)
  waiting for transfers between devices  7.35 us (13%)
  local copies, waits for them, and re-layouts  6.69 us (12%)
  other arithmetic  0.7 us (1%)
    ppermute x5, starting transfers between devices, shift(): return lax.ppermute(x, ('wear', 'age'), pairs)  13.1 us
    pallas_call x1, Pallas kernels, run_substeps(): pl.pallas_call(substeps_kernel, out_shape=jax.ShapeDtypeStruct(s.shape, f...  10.8 us
    pallas_call x1, Pallas kernels, section(): pl.pallas_call(functools.partial(section_kernel, ranks, sides), grid_spec...  8.97 us
    ppermute x4, starting transfers between devices, body(): lax.ppermute(x, 'cheb', list(pairs))  6.01 us
    unnamed x22, local copies, waits for them, and re-layouts  5.33 us
    ppermute x4, waiting for transfers between devices, body(): lax.ppermute(x, 'cheb', list(pairs))  4.43 us
    pallas_call x1, Pallas kernels, pack(): pl.pallas_call(functools.partial(pack_kernel, ranks), grid_spec=pltpu.Pre...  3.69 us
    ppermute x5, waiting for transfers between devices, shift(): return lax.ppermute(x, ('wear', 'age'), pairs)  2.92 us
  transfers between devices with their start and end apart: 9, of which 2 were waited for; matrix products, arithmetic and copies ran while one was open for 1% of the time, Pallas kernels for 0%

commit v1 on v0

v1 whole, which is shorter than its diff:
```python
import functools

import jax
import jax.numpy as jnp
import numpy as np
from jax import lax
from jax.experimental import pallas as pl
from jax.experimental.pallas import tpu as pltpu
from jax.sharding import PartitionSpec as P

SUBSTEPS = 4
HALO = SUBSTEPS

age_courant = 0.4
wear_spread = 0.1
coupling = 0.05
GAIN = 1.0 / coupling
START = coupling**SUBSTEPS

f32 = jnp.float32
bf16 = jnp.bfloat16
VMEM_LIMIT = 48 * 2**20


def operators(points):
    modes = np.arange(points)[:, None]
    nodes = np.arange(points)[None, :]
    angles = (modes * (2 * nodes + 1)) % (4 * points) * (np.pi / (2 * points))
    cosine, sine = np.cos(angles), np.sin(angles)
    analysis = np.where(modes == 0, 1.0, 2.0) / points * cosine
    wavenumber = modes / points
    return (-(wavenumber**2) * cosine).T @ analysis, (wavenumber * sine).T @ analysis


def arrived_rows(rank):
    return -(-rank // 16) * 16


@functools.lru_cache(maxsize=None)
def factors(points, devices):
    second, first = operators(points)
    size = points // devices
    parts = [slice(b * size, (b + 1) * size) for b in range(devices)]
    slots, found = [], {}
    for shift in range(1, devices):
        groups = {}
        for c in range(devices):
            b = c ^ shift if devices & (devices - 1) == 0 else (c + shift) % devices
            joint = np.concatenate([second[parts[b], parts[c]], first[parts[b], parts[c]]])
            _, sizes, rows = np.linalg.svd(joint, full_matrices=False)
            rank = int((sizes > joint.shape[0] * np.finfo(np.float64).eps).sum())
            rank = -(-rank // 8) * 8
            basis = rows[:rank]
            found[c, b] = (basis, second[parts[b], parts[c]] @ basis.T, first[parts[b], parts[c]] @ basis.T)
            groups.setdefault(rank, []).append((c, b))
        slots += [(tuple(pairs), rank) for rank, pairs in sorted(groups.items())]
    send = np.zeros((devices, sum(rank for _, rank in slots), size))
    wide = sum(arrived_rows(rank) for _, rank in slots)
    take_second = np.zeros((devices, 2, wide, size))
    take_first = np.zeros((devices, 2, wide, size))
    at = row = 0
    for pairs, rank in slots:
        whole = rank // 16 * 16
        for c, b in pairs:
            basis, left_second, left_first = found[c, b]
            send[c, at : at + rank] = basis
            for half in range(2):
                for take, left in ((take_second, left_second.T), (take_first, left_first.T)):
                    take[b, half, row : row + whole] = left[:whole]
                    place = row + whole + half * (rank - whole)
                    take[b, half, place : place + rank - whole] = left[whole:]
        at += rank
        row += arrived_rows(rank)
    own_second = np.stack([second[p, p].T for p in parts])
    own_first = np.stack([first[p, p].T for p in parts])
    return slots, send, take_second, take_first, own_second, own_first


def pack_kernel(ranks, at_ref, u_hbm, send_hbm, *refs):
    q_refs, (u_ref, send, send_sem, u_sem) = refs[: len(ranks)], refs[len(ranks) :]
    _, wears, ages, size = u_ref.shape
    chunk = 4
    table = pltpu.make_async_copy(send_hbm.at[at_ref[0]], send, send_sem)
    table.start()
    loads = []
    for g in range(wears // chunk):
        rows = pl.ds(g * chunk, chunk)
        loads.append(pltpu.make_async_copy(u_hbm.at[:, rows], u_ref.at[:, rows], u_sem.at[g]))
        loads[-1].start()
    table.wait()
    for g in range(wears // chunk):
        loads[g].wait()
        halves = []
        for half in range(2):
            cells = u_ref[half, g * chunk : (g + 1) * chunk].reshape(chunk * ages, size).astype(bf16)
            halves.append(
                lax.dot_general(send[...], cells, (((1,), (1,)), ((), ())), preferred_element_type=f32)
            )
        row = 0
        for rank, q_ref in zip(ranks, q_refs):
            cut = row + rank // 16 * 16
            pieces = [h[row:cut] for h in halves if cut > row] + [h[cut : row + rank] for h in halves if cut < row + rank]
            q_ref[:, g * chunk * ages : (g + 1) * chunk * ages] = jnp.concatenate(pieces, axis=0).astype(bf16)
            row += rank


ANY = pl.BlockSpec(memory_space=pl.ANY)
VMEM = pl.BlockSpec(memory_space=pltpu.VMEM)
SMEM = pl.BlockSpec(memory_space=pltpu.SMEM)


def in_hbm(x):
    return pltpu.with_memory_space_constraint(x, pltpu.HBM)


def pack(at, u4, send, ranks):
    _, wears, ages, size = u4.shape
    cells = wears * ages
    return pl.pallas_call(
        functools.partial(pack_kernel, ranks),
        in_specs=[SMEM, ANY, ANY],
        out_specs=[VMEM] * (len(ranks) + 1),
        out_shape=[jax.ShapeDtypeStruct((2 * r, cells), bf16) for r in ranks] + [pltpu.VMEM(u4.shape, f32)],
        scratch_shapes=[
            pltpu.VMEM(send.shape[1:], bf16),
            pltpu.SemaphoreType.DMA,
            pltpu.SemaphoreType.DMA((wears // 4,)),
        ],
        compiler_params=pltpu.CompilerParams(vmem_limit_bytes=16 * 2**20),
        cost_estimate=pl.CostEstimate(
            flops=4 * cells * sum(ranks) * size, bytes_accessed=8 * cells * size, transcendentals=0
        ),
        name="pack_coefficients",
    )(at, in_hbm(u4), in_hbm(send))


ROW0 = 16


def local_kernel(at_ref, u_ref, hazard_ref, diffusion_ref, drift_ref, second_hbm, first_hbm, z, second, first, own, sem):
    halves, rows, _, _ = z.shape
    _, wears, ages, size = u_ref.shape
    at = at_ref[0]
    copies = [
        pltpu.make_async_copy(second_hbm.at[at], second, sem.at[0]),
        pltpu.make_async_copy(first_hbm.at[at], first, sem.at[1]),
    ]
    for copy in copies:
        copy.start()
    for l in range(halves):
        zero = jnp.zeros((rows, 16, 128), f32)
        z[l, :, :ROW0, :] = zero
        z[l, :, ROW0 + ages :, :] = zero
    keep = jnp.transpose(START - START * hazard_ref[...])
    for copy in copies:
        copy.wait()
    own[...] = (second[...] * (START * diffusion_ref[at]) + first[...] * (START * drift_ref[at])).astype(bf16)
    chunk = 4
    for w in range(0, 2 * wears, chunk):
        half, v = divmod(w, wears)
        u = u_ref[half, v : v + chunk].reshape(chunk * ages, size)
        rate = jnp.dot(u.astype(bf16), own[...], preferred_element_type=f32)
        for i in range(chunk):
            cells = slice(i * ages, (i + 1) * ages)
            value = rate[cells] + keep[:, w + i : w + i + 1] * u[cells]
            for l in range(halves):
                z[l, HALO + w + i, ROW0 : ROW0 + ages, :] = value[:, l * 128 : (l + 1) * 128]


def local(at, u4, hazard, diffusion, drift, second, first):
    _, wears, ages, size = u4.shape
    cells = 2 * wears * ages
    return pl.pallas_call(
        local_kernel,
        in_specs=[SMEM] + [VMEM] * 4 + [ANY, ANY],
        out_specs=VMEM,
        out_shape=pltpu.VMEM((size // 128, 2 * wears + 2 * HALO, ages + 32, 128), f32),
        scratch_shapes=[
            pltpu.VMEM((size, size), f32),
            pltpu.VMEM((size, size), f32),
            pltpu.VMEM((size, size), bf16),
            pltpu.SemaphoreType.DMA((2,)),
        ],
        compiler_params=pltpu.CompilerParams(vmem_limit_bytes=24 * 2**20),
        cost_estimate=pl.CostEstimate(
            flops=2 * cells * size * size, bytes_accessed=8 * cells * size, transcendentals=0
        ),
        name="local_rate",
    )(at, u4, hazard, diffusion, drift, in_hbm(second), in_hbm(first))


def section_kernel(ranks, sides, wears, ages, at_ref, side_ref, z_in, diffusion_ref, drift_ref, second_hbm, first_hbm,
                   *refs):
    q_refs, refs = refs[: len(ranks)], refs[len(ranks) :]
    z, top_ref, bottom_ref = refs[:3]
    edge_refs = refs[3 : 3 + sides]
    second, first, take, sem = refs[3 + sides :]
    halves, size = z.shape[0], z.shape[0] * 128
    at = at_ref[0]
    copies = [
        pltpu.make_async_copy(second_hbm.at[at], second, sem.at[0]),
        pltpu.make_async_copy(first_hbm.at[at], first, sem.at[1]),
    ]
    for copy in copies:
        copy.start()
    for copy in copies:
        copy.wait()
    take[...] = (second[...] * (START * diffusion_ref[at]) + first[...] * (START * drift_ref[at])).astype(bf16)
    chunk = 4
    for w in range(0, wears, chunk):
        half, v = divmod(w, wears // 2)
        columns = slice(v * ages, (v + chunk) * ages)
        tiles = []
        for rank, q in zip(ranks, q_refs):
            cut = rank // 16 * 16
            if cut:
                tiles.append(q[half * cut : (half + 1) * cut, columns])
            if rank > cut:
                tiles.append(q[2 * cut : 2 * rank, columns])
        rate = lax.dot_general(
            jnp.concatenate(tiles, axis=0), take[half], (((0,), (0,)), ((), ())), preferred_element_type=f32
        )
        values = []
        for i in range(chunk):
            value = [
                z_in[l, HALO + w + i, ROW0 : ROW0 + ages, :]
                + rate[i * ages : (i + 1) * ages, l * 128 : (l + 1) * 128]
                for l in range(halves)
            ]
            for l in range(halves):
                z[l, HALO + w + i, ROW0 : ROW0 + ages, :] = value[l]
            values.append(jnp.concatenate(value, axis=1))
        last = jnp.concatenate([x[ages - HALO :] for x in values], axis=0)
        early = jnp.concatenate([x[:HALO] for x in values], axis=0)
        place = slice(v * HALO, (v + chunk) * HALO)
        if sides == 1:
            edge_refs[0][half, place] = jnp.where(side_ref[0] == 0, last, early).astype(bf16)
        else:
            edge_refs[0][half, place] = last.astype(bf16)
            edge_refs[1][half, place] = early.astype(bf16)
        for start, ref in ((0, top_ref), (wears - HALO, bottom_ref)):
            if w == start:
                ref[...] = jnp.concatenate(values, axis=0).astype(bf16)


def section(at, side, z, diffusion, drift, second, first, q, ranks, sides, wears, ages):
    size = z.shape[0] * 128
    cells = wears * ages
    wide = second.shape[2]
    return pl.pallas_call(
        functools.partial(section_kernel, ranks, sides, wears, ages),
        in_specs=[SMEM, SMEM, VMEM, VMEM, VMEM, ANY, ANY] + [VMEM] * len(ranks),
        out_specs=[VMEM] * (3 + sides),
        out_shape=[
            pltpu.VMEM(z.shape, f32),
            jax.ShapeDtypeStruct((HALO * ages, size), bf16),
            jax.ShapeDtypeStruct((HALO * ages, size), bf16),
        ]
        + [jax.ShapeDtypeStruct((2, wears // 2 * HALO, size), bf16)] * sides,
        scratch_shapes=[
            pltpu.VMEM((2, wide, size), f32),
            pltpu.VMEM((2, wide, size), f32),
            pltpu.VMEM((2, wide, size), bf16),
            pltpu.SemaphoreType.DMA((2,)),
        ],
        input_output_aliases={2: 0},
        compiler_params=pltpu.CompilerParams(vmem_limit_bytes=24 * 2**20),
        cost_estimate=pl.CostEstimate(
            flops=2 * cells * wide * size, bytes_accessed=8 * cells * size, transcendentals=0
        ),
        name="section",
    )(at, side, z, diffusion, drift, in_hbm(second), in_hbm(first), *q)


def substeps_kernel(flag_ref, z_in, speed_ref, up_ref, down_ref, left_ref, right_ref, ul_ref, ur_ref, dl_ref,
                    dr_ref, o_ref, za, zb, stage, out_sem):
    halves, rows, _, _ = za.shape
    wears, ages = rows - 2 * HALO, stage.shape[1]
    first_w, last_w, first_a, last_a = (flag_ref[i] == 1 for i in range(4))
    low, high = ROW0 - 8, ROW0 + ages + 8
    has_left = jnp.where(first_a, 0.0, 1.0).astype(f32)
    has_right = jnp.where(last_a, 0.0, 1.0).astype(f32)
    for l in range(halves):
        lanes = pl.ds(l * 128, 128)
        zero = jnp.zeros((rows, 8, 128), f32)
        zb[l, :, low - 8 : low, :] = zero
        zb[l, :, high : high + 8, :] = zero
        for ref, at in ((up_ref, 0), (down_ref, HALO + wears)):
            za[l, at : at + HALO, ROW0 : ROW0 + ages, :] = ref[:, lanes].astype(f32).reshape(HALO, ages, 128)
        for ref, at, count, col, has in (
            (left_ref, HALO, wears, ROW0 - HALO, has_left),
            (right_ref, HALO, wears, ROW0 + ages, has_right),
            (ul_ref, 0, HALO, ROW0 - HALO, has_left),
            (ur_ref, 0, HALO, ROW0 + ages, has_right),
            (dl_ref, HALO + wears, HALO, ROW0 - HALO, has_left),
            (dr_ref, HALO + wears, HALO, ROW0 + ages, has_right),
        ):
            strip = ref[:, lanes].astype(f32) * has
            za[l, at : at + count, col : col + HALO, :] = strip.reshape(count, HALO, 128)

    keep_low = jnp.zeros((8, 128), f32) + has_left
    keep_high = jnp.zeros((8, 128), f32) + has_right
    stores = []
    for k in range(1, SUBSTEPS + 1):
        src, dst = (za, zb) if k % 2 == 1 else (zb, za)
        final = k == SUBSTEPS
        lo, hi = (ROW0, ROW0 + ages) if final else (low, high)
        pieces = 4 if final else 1
        bounds = [k + (rows - 2 * k) * p // pieces for p in range(pieces + 1)]
        for p in range(pieces):
            for l in range(halves):
                speed = speed_ref[0:1, l * 128 : (l + 1) * 128]
                stay = GAIN * (1.0 - age_courant - 2.0 * wear_spread - speed)
                worn = GAIN * (speed + wear_spread)

                def terms(w, src=src, l=l, lo=lo, hi=hi, stay=stay, worn=worn):
                    t = src[l, w, lo:hi, :]
                    older = src[l, w, lo + 1 : hi + 1, :]
                    slope = older - src[l, w, lo - 1 : hi - 1, :]
                    centre = stay * t + (GAIN * age_courant) * older
                    less = (t - slope) + t
                    return centre, worn * t + slope, less

                def body(w, carry, dst=dst, l=l, lo=lo, hi=hi, final=final, terms=terms):
                    partial, less = carry
                    centre, more, new_less = terms(w + 1)
                    out = partial + more
                    if final:
                        stage[w - HALO, :, l * 128 : (l + 1) * 128] = out
                    else:
                        dst[l, w, lo : lo + 8, :] = out[:8] * keep_low
                        dst[l, w, lo + 8 : hi - 8, :] = out[8:-8]
                        dst[l, w, hi - 8 : hi, :] = out[-8:] * keep_high
                    return centre + less, new_less

                start, stop = bounds[p], bounds[p + 1]
                _, _, less0 = terms(start - 1)
                centre1, _, less1 = terms(start)
                count = stop - start
                lax.fori_loop(start, stop, body, (centre1 + less0, less1), unroll=4 if count % 4 == 0 else 2)
            if final:
                a, b = bounds[p] - HALO, bounds[p + 1] - HALO
                copy = pltpu.make_async_copy(
                    stage.at[pl.ds(a, b - a)], o_ref.at[pl.ds(a, b - a)], out_sem.at[p]
                )
                copy.start()
                stores.append(copy)
        if not final:
            for at, flag in ((HALO - 1, first_w), (HALO + wears, last_w)):
                @pl.when(flag)
                def _(dst=dst, at=at):
                    for l in range(halves):
                        dst[l, at, low:high, :] = jnp.zeros((high - low, 128), f32)
    for copy in stores:
        copy.wait()


def run_substeps(flags, z, speed, halos, wears, ages):
    size = z.shape[0] * 128
    shape = (wears, ages, size)
    return pl.pallas_call(
        substeps_kernel,
        out_shape=[jax.ShapeDtypeStruct(shape, f32), pltpu.VMEM(z.shape, f32)],
        in_specs=[SMEM] + [VMEM] * 10,
        out_specs=[ANY, VMEM],
        scratch_shapes=[
            pltpu.VMEM(z.shape, f32),
            pltpu.VMEM(shape, f32),
            pltpu.SemaphoreType.DMA((4,)),
        ],
        input_output_aliases={1: 1},
        compiler_params=pltpu.CompilerParams(vmem_limit_bytes=32 * 2**20),
        cost_estimate=pl.CostEstimate(
            flops=10 * SUBSTEPS * wears * ages * size, bytes_accessed=8 * wears * ages * size, transcendentals=0
        ),
        name="substeps",
    )(flags, z, speed, *halos)[0]


def body(adjoint_value, load_diffusion, load_drift, wear_speed, hazard):
    wears, ages, size = adjoint_value.shape
    points = load_diffusion.shape[0]
    devices = points // size
    slots, send, take_second, take_first, own_second, own_first = factors(points, devices)
    ranks = tuple(rank for _, rank in slots)
    cheb = lax.axis_index("cheb")
    wear, age = lax.axis_index("wear"), lax.axis_index("age")
    n_wear, n_age = lax.axis_size("wear"), lax.axis_size("age")
    at = cheb.astype(jnp.int32).reshape(1)
    side = age.astype(jnp.int32).reshape(1)
    u4 = adjoint_value.reshape(2, wears // 2, ages, size)
    diffusion = load_diffusion.reshape(devices, 1, size)
    drift = load_drift.reshape(devices, 1, size)

    *q, u4 = pack(at, u4, jnp.asarray(send, bf16), ranks)
    arrived = [lax.ppermute(x, "cheb", list(pairs)) for x, (pairs, _) in zip(q, slots)]
    z = local(at, u4, hazard, diffusion, drift, jnp.asarray(own_second, f32), jnp.asarray(own_first, f32))
    sides = 1 if n_age == 2 else 2
    z, top, bottom, *edges = section(
        at, side, z, diffusion, drift, jnp.asarray(take_second, f32), jnp.asarray(take_first, f32), arrived, ranks,
        sides, wears, ages,
    )
    corner = HALO * HALO

    def shift(x, dw, da):
        pairs = []
        for w in range(n_wear):
            for a in range(n_age):
                to_w, to_a = w + dw, (1 - a if da is None else a + da)
                if 0 <= to_w < n_wear and 0 <= to_a < n_age:
                    pairs.append((w * n_age + a, to_w * n_age + to_a))
        return lax.ppermute(x, ("wear", "age"), pairs)

    if sides == 1:
        x = edges[0]
        ul = ur = shift(x[1, -corner:], 1, None)
        dl = dr = shift(x[0, :corner], -1, None)
        left = right = shift(x, 0, None).reshape(-1, size)
    else:
        last, first = edges
        ul, ur = shift(last[1, -corner:], 1, 1), shift(first[1, -corner:], 1, -1)
        dl, dr = shift(last[0, :corner], -1, 1), shift(first[0, :corner], -1, -1)
        left, right = shift(last, 0, 1).reshape(-1, size), shift(first, 0, -1).reshape(-1, size)
    up, down = shift(bottom, 1, 0), shift(top, -1, 0)
    flags = jnp.stack([wear == 0, wear == n_wear - 1, age == 0, age == n_age - 1]).astype(jnp.int32)
    halos = [up, down, left, right, ul, ur, dl, dr]
    return run_substeps(flags, z, wear_speed.reshape(1, size), halos, wears, ages)


def solution(mesh):
    placed = (P("wear", "age", "cheb"), P(), P(), P("cheb"), P("wear", "age"))
    return jax.shard_map(
        body, mesh=mesh, in_specs=placed, out_specs=P("wear", "age", "cheb"), check_vma=False
    )
```

time: 58.1 us -> 47.8 us (0.82)
  the two profiles are of different devices: /device:TPU:22 before, /device:TPU:0 now
where the time goes in v1:
time: 47.8 us; the launch traced here: 47.1 us
  starting transfers between devices  21.3 us (45%)
  Pallas kernels  17.9 us (37%)
  local copies, waits for them, and re-layouts  6.33 us (13%)
  waiting for transfers between devices  1.29 us (3%)
    ppermute x5, starting transfers between devices, shift(): return lax.ppermute(x, ('wear', 'age'), pairs)  13.1 us
    pallas_call x1, Pallas kernels, run_substeps(): pl.pallas_call(substeps_kernel, out_shape=[jax.ShapeDtypeStruct(shape, f3...  10.3 us
    ppermute x4, starting transfers between devices, body(): lax.ppermute(x, 'cheb', list(pairs))  8.29 us
    unnamed x12, local copies, waits for them, and re-layouts  6.33 us
    pallas_call x1, Pallas kernels, pack(): pl.pallas_call(functools.partial(pack_kernel, ranks), in_specs=[SMEM, ANY...  3.63 us
    pallas_call x1, Pallas kernels, section(): pl.pallas_call(functools.partial(section_kernel, ranks, sides, wears, age...  2.16 us
    pallas_call x1, Pallas kernels, local(): pl.pallas_call(local_kernel, in_specs=[SMEM] + [VMEM] * 4 + [ANY, ANY], o...  1.85 us
    ppermute x5, waiting for transfers between devices, shift(): return lax.ppermute(x, ('wear', 'age'), pairs)  1.28 us
  transfers between devices with their start and end apart: 9, of which 1 were waited for; matrix products, arithmetic and copies ran while one was open for 0% of the time, Pallas kernels for 4%

profile of v1, /device:TPU:0, one launch (start us, length us, event | category | flops | bytes accessed | tf_op | source)
XLA Modules:
  0.0 47.1 jit_solution(13741828222385503142)
XLA Ops:
  0.0 3.6 %pack_coefficients.1 = (bf16[48,2048]{1,0:T(8,128)(2,1)S(1)}, bf16[16,2048]{1,0:T(8,128)(2,1)S(1)}, bf16[16,2048]{1,0:T(8,128)(2,1)S(1)}, bf16[48,2048]{1,0:T(8,128)(2,1)S(1)}, f32[2,32,64,256]{3,2,1,0:T(8,128)S(1)}) custom-call(s32[1]{0:T(128)} %bitcast.4.at_ref, f32[2,32,64,256]{3,2,1,0:T(8,128)} %bitcast.22, bf16[4,64,256]{2,1,0:T(8,128)(2,1)} %constant.27.clone.send_hbm), custom_call_target="tpu_custom_call" | custom-call | flops 134217728 | bytes 4194304 | tf_op jit(solution)/shard_map/pack_coefficients/pallas_call | solution.py:119
  3.6 0.0 copy-start
  3.7 2.0 %copy-done = f32[2,32,64,256]{3,2,1,0:T(8,128)} copy-done((f32[2,32,64,256]{3,2,1,0:T(8,128)}, f32[2,32,64,256]{3,2,1,0:T(8,128)S(1)}, u32[]{:S(2)}) %copy-start) | copy-done | bytes 4194328
  5.7 0.5 collective-permute-start
  6.1 0.7 %collective-permute-start.3 = (bf16[48,2048]{1,0:T(8,128)(2,1)S(1)}, bf16[48,2048]{1,0:T(8,128)(2,1)S(1)}, u32[]{:S(2)}, u32[]{:S(2)}) collective-permute-start(bf16[48,2048]{1,0:T(8,128)(2,1)S(1)} %get-tuple-element.19), channel_id=1, source_target_pairs={{8,16},{16,8},{9,17},{17,9},{10,18},{18,10},{11,19},{19,11},{12,20... | collective-permute-start | bytes 589832 | tf_op jit(solution)/shard_map/ppermute | solution.py:396
  6.8 3.8 %collective-permute-start.1 = (bf16[16,2048]{1,0:T(8,128)(2,1)S(1)}, bf16[16,2048]{1,0:T(8,128)(2,1)S(1)}, u32[]{:S(2)}, u32[]{:S(2)}) collective-permute-start(bf16[16,2048]{1,0:T(8,128)(2,1)S(1)} %get-tuple-element.17), channel_id=1, source_target_pairs={{0,16},{8,24},{16,0},{24,8},{1,17},{9,25},{17,1},{25,9},{2,18},{10... | collective-permute-start | bytes 196616 | tf_op jit(solution)/shard_map/ppermute | solution.py:396
  10.6 3.4 %collective-permute-start.2 = (bf16[16,2048]{1,0:T(8,128)(2,1)S(1)}, bf16[16,2048]{1,0:T(8,128)(2,1)S(1)}, u32[]{:S(2)}, u32[]{:S(2)}) collective-permute-start(bf16[16,2048]{1,0:T(8,128)(2,1)S(1)} %get-tuple-element.18), channel_id=1, source_target_pairs={{0,24},{24,0},{1,25},{25,1},{2,26},{26,2},{3,27},{27,3},{4,28},{28... | collective-permute-start | bytes 196616 | tf_op jit(solution)/shard_map/ppermute | solution.py:396
  14.0 0.0 copy-start.1
  14.0 2.2 %copy-done.1 = f32[2,32,64,256]{3,2,1,0:T(8,128)S(1)} copy-done((f32[2,32,64,256]{3,2,1,0:T(8,128)S(1)}, f32[2,32,64,256]{3,2,1,0:T(8,128)}, u32[]{:S(2)}) %copy-start.1) | copy-done | bytes 4194328
  16.2 0.0 copy-start.2
  16.2 0.8 %copy-done.2 = f32[64,64]{1,0:T(8,128)S(1)} copy-done((f32[64,64]{1,0:T(8,128)S(1)}, f32[64,64]{1,0:T(8,128)}, u32[]{:S(2)}) %copy-start.2) | copy-done | bytes 16408
  16.9 0.0 copy-start.3
  16.9 0.7 %copy-done.3 = f32[1024]{0:T(1024)S(1)} copy-done((f32[1024]{0:T(1024)S(1)}, f32[1024]{0:T(1024)}, u32[]{:S(2)}) %copy-start.3) | copy-done | bytes 4120
  17.6 0.0 copy-start.4
  17.6 0.7 %copy-done.4 = f32[1024]{0:T(1024)S(1)} copy-done((f32[1024]{0:T(1024)S(1)}, f32[1024]{0:T(1024)}, u32[]{:S(2)}) %copy-start.4) | copy-done | bytes 4120
  18.3 1.8 %local_rate.1.z_in = f32[2,72,96,128]{3,2,1,0:T(8,128)S(1)} custom-call(s32[1]{0:T(128)} %bitcast.4.at_ref, f32[2,32,64,256]{3,2,1,0:T(8,128)S(1)} %copy-done.1, f32[64,64]{1,0:T(8,128)S(1)} %copy-done.2, f32[4,1,256]{2,1,0:T(1,128)S(1)} %bitcast.17, f32[4,1,256]{2,1,0:T(1,128)S(1)} %bitcast.19, f32[4,256,256]{2,1,0:T(8,128)} %constant.28.clone.second_hbm, ...), custom_call_target="tpu_custom_call" | custom-call | flops 536870912 | bytes 8388608 | tf_op jit(solution)/shard_map/local_rate/pallas_call | solution.py:173
  20.2 0.0 copy-start.5
  20.2 0.0 collective-permute-done.1.refs_1_
  20.2 0.0 collective-permute-done.2.refs_2_
  20.2 0.0 collective-permute-done.refs_0_
  20.2 0.0 collective-permute-done.3.refs_3_
  20.2 2.2 %section.1 = (f32[2,72,96,128]{3,2,1,0:T(8,128)S(1)}, bf16[256,256]{1,0:T(8,128)(2,1)S(1)}, bf16[256,256]{1,0:T(8,128)(2,1)S(1)}, bf16[2,128,256]{2,1,0:T(8,128)(2,1)S(1)}) custom-call(s32[1]{0:T(128)} %bitcast.4.at_ref, s32[1]{0:T(128)} %bitcast.5.side_ref, f32[2,72,96,128]{3,2,1,0:T(8,128)S(1)} %local_rate.1.z_in, ...), custom_call_target="tpu_custom_call", output_to_operand_aliasing={{0}: (2, {})} | custom-call | flops 201326592 | bytes 8388608 | tf_op jit(solution)/shard_map/section/pallas_call | solution.py:250
  22.4 3.5 %collective-permute-start.4 = (bf16[256,256]{1,0:T(8,128)(2,1)S(1)}, bf16[256,256]{1,0:T(8,128)(2,1)S(1)}, u32[]{:S(2)}, u32[]{:S(2)}) collective-permute-start(bf16[256,256]{1,0:T(8,128)(2,1)S(1)} %get-tuple-element.21), channel_id=1, source_target_pairs={{0,2},{1,3},{2,4},{3,5},{4,6},{5,7},{8,10},{9,11},{10,12},{11,13},... | collective-permute-start | bytes 393224 | tf_op jit(solution)/shard_map/ppermute | solution.py:412
  25.9 1.3 %collective-permute-start.5 = (bf16[256,256]{1,0:T(8,128)(2,1)S(1)}, bf16[256,256]{1,0:T(8,128)(2,1)S(1)}, u32[]{:S(2)}, u32[]{:S(2)}) collective-permute-start(bf16[256,256]{1,0:T(8,128)(2,1)S(1)} %get-tuple-element.22), channel_id=1, source_target_pairs={{2,0},{3,1},{4,2},{5,3},{6,4},{7,5},{10,8},{11,9},{12,10},{13,11},... | collective-permute-start | bytes 393224 | tf_op jit(solution)/shard_map/ppermute | solution.py:412
  27.2 1.6 %collective-permute-start.6 = (bf16[2,128,256]{2,1,0:T(8,128)(2,1)S(1)}, bf16[2,128,256]{2,1,0:T(8,128)(2,1)S(1)}, u32[]{:S(2)}, u32[]{:S(2)}) collective-permute-start(bf16[2,128,256]{2,1,0:T(8,128)(2,1)S(1)} %get-tuple-element.23), channel_id=1, source_target_pairs={{0,1},{1,0},{2,3},{3,2},{4,5},{5,4},{6,7},{7,6},{8,9},{9,8},{10,11... | collective-permute-start | bytes 393224 | tf_op jit(solution)/shard_map/ppermute | solution.py:412
  28.7 1.3 %collective-permute-start.8 = (bf16[16,256]{1,0:T(8,128)(2,1)S(1)}, bf16[16,256]{1,0:T(8,128)(2,1)S(1)}, u32[]{:S(2)}, u32[]{:S(2)}) collective-permute-start(bf16[16,256]{1,0:T(8,128)(2,1)S(1)} %get-tuple-element.25), channel_id=1, source_target_pairs={{2,1},{3,0},{4,3},{5,2},{6,5},{7,4},{10,9},{11,8},{12,11},{13,10},... | collective-permute-start | bytes 24584 | tf_op jit(solution)/shard_map/ppermute | solution.py:412
  30.0 5.4 %collective-permute-start.7 = (bf16[16,256]{1,0:T(8,128)(2,1)S(1)}, bf16[16,256]{1,0:T(8,128)(2,1)S(1)}, u32[]{:S(2)}, u32[]{:S(2)}) collective-permute-start(bf16[16,256]{1,0:T(8,128)(2,1)S(1)} %get-tuple-element.26), channel_id=1, source_target_pairs={{0,3},{1,2},{2,5},{3,4},{4,7},{5,6},{8,11},{9,10},{10,13},{11,12},... | collective-permute-start | bytes 24584 | tf_op jit(solution)/shard_map/ppermute | solution.py:412
  35.5 0.1 add_convert_fusion.flag_ref
  35.5 0.0 collective-permute-done.8.dl_ref.dr_ref
  35.6 1.3 %collective-permute-done.7.ul_ref.ur_ref = bf16[16,256]{1,0:T(8,128)(2,1)S(1)} collective-permute-done((bf16[16,256]{1,0:T(8,128)(2,1)S(1)}, bf16[16,256]{1,0:T(8,128)(2,1)S(1)}, u32[]{:S(2)}, u32[]{:S(2)}) %collective-permute-start.7) | collective-permute-done | bytes 8224 | tf_op jit(solution)/shard_map/ppermute | solution.py:412
  36.8 0.0 collective-permute-done.4.up_ref
  36.8 0.0 collective-permute-done.5.down_ref
  36.8 0.0 collective-permute-done.6
  36.8 0.0 copy-done.5
  36.8 10.3 %substeps.1 = (f32[64,64,256]{2,1,0:T(8,128)}, f32[2,72,96,128]{3,2,1,0:T(8,128)S(1)}) custom-call(s32[4]{0:T(128)S(1)} %add_convert_fusion.flag_ref, f32[2,72,96,128]{3,2,1,0:T(8,128)S(1)} %get-tuple-element.20.z_in, f32[1,256]{1,0:T(1,128)S(1)} %bitcast.21, bf16[256,256]{1,0:T(8,128)(2,1)S(1)} %collective-permute-done.4.up_ref, ...), custom_call_target="tpu_custom_call", output_to_operand_aliasing={{1}: (1, {})} | custom-call | flops 41943040 | bytes 8388608 | tf_op jit(solution)/shard_map/substeps/pallas_call | solution.py:361
  (1 shorter events, 0.0 us)
Async XLA Ops:
  3.6 2.0 %copy-start = (f32[2,32,64,256]{3,2,1,0:T(8,128)}, f32[2,32,64,256]{3,2,1,0:T(8,128)S(1)}, u32[]{:S(2)}) copy-start(f32[2,32,64,256]{3,2,1,0:T(8,128)S(1)} %get-tuple-element.15.u_ref) | copy-start | bytes 12582916
  5.7 14.5 %collective-permute-start = (bf16[48,2048]{1,0:T(8,128)(2,1)S(1)}, bf16[48,2048]{1,0:T(8,128)(2,1)S(1)}, u32[]{:S(2)}, u32[]{:S(2)}) collective-permute-start(bf16[48,2048]{1,0:T(8,128)(2,1)S(1)} %get-tuple-element.16), channel_id=1, source_target_pairs={{0,8},{8,0},{16,24},{24,16},{1,9},{9,1},{17,25},{25,17},{2,10},{10... | collective-permute-start | bytes 589832 | tf_op jit(solution)/shard_map/ppermute | solution.py:396
  6.1 14.1 %collective-permute-start.3 = (bf16[48,2048]{1,0:T(8,128)(2,1)S(1)}, bf16[48,2048]{1,0:T(8,128)(2,1)S(1)}, u32[]{:S(2)}, u32[]{:S(2)}) collective-permute-start(bf16[48,2048]{1,0:T(8,128)(2,1)S(1)} %get-tuple-element.19), channel_id=1, source_target_pairs={{8,16},{16,8},{9,17},{17,9},{10,18},{18,10},{11,19},{19,11},{12,20... | collective-permute-start | bytes 589832 | tf_op jit(solution)/shard_map/ppermute | solution.py:396
  6.8 13.4 %collective-permute-start.1 = (bf16[16,2048]{1,0:T(8,128)(2,1)S(1)}, bf16[16,2048]{1,0:T(8,128)(2,1)S(1)}, u32[]{:S(2)}, u32[]{:S(2)}) collective-permute-start(bf16[16,2048]{1,0:T(8,128)(2,1)S(1)} %get-tuple-element.17), channel_id=1, source_target_pairs={{0,16},{8,24},{16,0},{24,8},{1,17},{9,25},{17,1},{25,9},{2,18},{10... | collective-permute-start | bytes 196616 | tf_op jit(solution)/shard_map/ppermute | solution.py:396
  10.6 9.6 %collective-permute-start.2 = (bf16[16,2048]{1,0:T(8,128)(2,1)S(1)}, bf16[16,2048]{1,0:T(8,128)(2,1)S(1)}, u32[]{:S(2)}, u32[]{:S(2)}) collective-permute-start(bf16[16,2048]{1,0:T(8,128)(2,1)S(1)} %get-tuple-element.18), channel_id=1, source_target_pairs={{0,24},{24,0},{1,25},{25,1},{2,26},{26,2},{3,27},{27,3},{4,28},{28... | collective-permute-start | bytes 196616 | tf_op jit(solution)/shard_map/ppermute | solution.py:396
  14.0 2.2 %copy-start.1 = (f32[2,32,64,256]{3,2,1,0:T(8,128)S(1)}, f32[2,32,64,256]{3,2,1,0:T(8,128)}, u32[]{:S(2)}) copy-start(f32[2,32,64,256]{3,2,1,0:T(8,128)} %copy-done) | copy-start | bytes 12582916
  16.2 0.8 %copy-start.2 = (f32[64,64]{1,0:T(8,128)S(1)}, f32[64,64]{1,0:T(8,128)}, u32[]{:S(2)}) copy-start(f32[64,64]{1,0:T(8,128)} %hazard_ref.1) | copy-start | bytes 49156
  16.9 0.7 %copy-start.3 = (f32[1024]{0:T(1024)S(1)}, f32[1024]{0:T(1024)}, u32[]{:S(2)}) copy-start(f32[1024]{0:T(1024)} %param.11) | copy-start | bytes 12292
  17.6 0.7 %copy-start.4 = (f32[1024]{0:T(1024)S(1)}, f32[1024]{0:T(1024)}, u32[]{:S(2)}) copy-start(f32[1024]{0:T(1024)} %param.12) | copy-start | bytes 12292
  20.2 16.7 %copy-start.5 = (f32[256]{0:T(256)S(1)}, f32[256]{0:T(256)}, u32[]{:S(2)}) copy-start(f32[256]{0:T(256)} %param.13) | copy-start | bytes 3076
  22.4 14.4 %collective-permute-start.4 = (bf16[256,256]{1,0:T(8,128)(2,1)S(1)}, bf16[256,256]{1,0:T(8,128)(2,1)S(1)}, u32[]{:S(2)}, u32[]{:S(2)}) collective-permute-start(bf16[256,256]{1,0:T(8,128)(2,1)S(1)} %get-tuple-element.21), channel_id=1, source_target_pairs={{0,2},{1,3},{2,4},{3,5},{4,6},{5,7},{8,10},{9,11},{10,12},{11,13},... | collective-permute-start | bytes 393224 | tf_op jit(solution)/shard_map/ppermute | solution.py:412
  25.9 11.0 %collective-permute-start.5 = (bf16[256,256]{1,0:T(8,128)(2,1)S(1)}, bf16[256,256]{1,0:T(8,128)(2,1)S(1)}, u32[]{:S(2)}, u32[]{:S(2)}) collective-permute-start(bf16[256,256]{1,0:T(8,128)(2,1)S(1)} %get-tuple-element.22), channel_id=1, source_target_pairs={{2,0},{3,1},{4,2},{5,3},{6,4},{7,5},{10,8},{11,9},{12,10},{13,11},... | collective-permute-start | bytes 393224 | tf_op jit(solution)/shard_map/ppermute | solution.py:412
  27.2 9.7 %collective-permute-start.6 = (bf16[2,128,256]{2,1,0:T(8,128)(2,1)S(1)}, bf16[2,128,256]{2,1,0:T(8,128)(2,1)S(1)}, u32[]{:S(2)}, u32[]{:S(2)}) collective-permute-start(bf16[2,128,256]{2,1,0:T(8,128)(2,1)S(1)} %get-tuple-element.23), channel_id=1, source_target_pairs={{0,1},{1,0},{2,3},{3,2},{4,5},{5,4},{6,7},{7,6},{8,9},{9,8},{10,11... | collective-permute-start | bytes 393224 | tf_op jit(solution)/shard_map/ppermute | solution.py:412
  28.7 6.8 %collective-permute-start.8 = (bf16[16,256]{1,0:T(8,128)(2,1)S(1)}, bf16[16,256]{1,0:T(8,128)(2,1)S(1)}, u32[]{:S(2)}, u32[]{:S(2)}) collective-permute-start(bf16[16,256]{1,0:T(8,128)(2,1)S(1)} %get-tuple-element.25), channel_id=1, source_target_pairs={{2,1},{3,0},{4,3},{5,2},{6,5},{7,4},{10,9},{11,8},{12,11},{13,10},... | collective-permute-start | bytes 24584 | tf_op jit(solution)/shard_map/ppermute | solution.py:412
  30.0 6.8 %collective-permute-start.7 = (bf16[16,256]{1,0:T(8,128)(2,1)S(1)}, bf16[16,256]{1,0:T(8,128)(2,1)S(1)}, u32[]{:S(2)}, u32[]{:S(2)}) collective-permute-start(bf16[16,256]{1,0:T(8,128)(2,1)S(1)} %get-tuple-element.26), channel_id=1, source_target_pairs={{0,3},{1,2},{2,5},{3,4},{4,7},{5,6},{8,11},{9,10},{10,13},{11,12},... | collective-permute-start | bytes 24584 | tf_op jit(solution)/shard_map/ppermute | solution.py:412
